TPU v7x, 32 devices: a whole 2x2x4 slice. The times are simulated.
32 devices in a mesh: groups: 2 (over y), replica: 4 (over z), tensor: 4 (over x, core).
Axes of the slice: x: 2, y: 2, z: 4, core: 2. Of those that a mesh axis runs over, the one named last changes fastest.
Arguments:
- normed_hidden_rows: bfloat16 [24576, 8192], P(('groups', 'replica'), 'tensor'), parts along dimension 0, may hold values from -6 to 6
- block_adapter_index: int32 [192], P(('groups', 'replica')), parts along dimension 0, may hold values from 0 to 3
- transfer_plan: int32 [64, 2], P('groups'), parts along dimension 0, may hold values from -1 to 23, as said below
- key_value_weight: bfloat16 [8192, 2048], P('tensor'), may hold values from -0.0625 to 0.0625
- adapter_down_weight: bfloat16 [32, 64, 8192], P(('groups', 'replica'), None, 'tensor'), parts along dimension 0, may hold values from -0.0625 to 0.0625
- adapter_up_weight: bfloat16 [32, 64, 2048], P(('groups', 'replica'), None, 'tensor'), parts along dimension 0, may hold values from -0.75 to 0.75
Outputs:
- kv_out: bfloat16 [8192, 2048], P(('groups', 'replica'), 'tensor'), parts along dimension 0
There are 2 independent parts, one for each index of `groups`. A program takes and returns all parts, laid end to end along the dimension named above; an argument that names none is the same for every part. Nothing has to cross between parts.
Inputs may be any that keep to these rules, and one draw needn't show every extreme that they name: `transfer_plan`: row d * 8 + j is slot j of replica d: column 0 a source replica, column 1 one of that replica's 24 blocks, both -1 in an empty slot. No block appears twice. One source fills at most 6 slots of one replica, and some source fills exactly 6 of some replica. Some replica has all 8 slots filled. Exactly one replica has all 24 of its blocks in the plan.
All inputs are finite; a program needn't handle non-finite values.
Results may differ from a plain program's by a relative error of at most 0.0029.
Values may be sent and summed in bfloat16 or wider, within the bound.
A program may use at most 128 MiB of HBM per device.

v0:
```python
import jax
import jax.numpy as jnp
from jax import lax
from jax.sharding import PartitionSpec as P

adapter_scale = 0.5


def shards(
    normed_hidden_rows,
    block_adapter_index,
    transfer_plan,
    key_value_weight,
    adapter_down_weight,
    adapter_up_weight,
):
    replicas = lax.axis_size("replica")
    myself = lax.axis_index("replica")
    replica_slot_count = transfer_plan.shape[0] // replicas
    pair_cap = (3 * replica_slot_count + replicas - 1) // replicas
    home_count = block_adapter_index.shape[0]
    queued_block_rows = normed_hidden_rows.shape[0] // home_count
    width_dev = normed_hidden_rows.shape[1]
    home_rows = normed_hidden_rows.reshape(home_count, queued_block_rows, width_dev)
    source = transfer_plan[:, 0].reshape(replicas, replica_slot_count)
    block_of = transfer_plan[:, 1].reshape(replicas, replica_slot_count)
    slot_ids = jnp.arange(replica_slot_count)
    earlier = slot_ids[None, :, None] > slot_ids[None, None, :]
    same_source = source[:, :, None] == source[:, None, :]
    order_rank = jnp.sum(same_source & earlier, axis=2)
    lane_ids = jnp.arange(pair_cap)
    outgoing = (source == myself)[:, None, :] & (order_rank[:, None, :] == lane_ids[None, :, None])
    sent_block = jnp.sum(jnp.where(outgoing, block_of[:, None, :], 0), axis=2).reshape(-1)
    sent_live = jnp.any(outgoing, axis=2).reshape(-1)
    home_ids = jnp.arange(home_count)
    pick_home = (sent_live[:, None] & (sent_block[:, None] == home_ids[None, :])).astype(
        jnp.bfloat16
    )
    replica_adapter = (
        block_adapter_index[:, None] == jnp.arange(adapter_down_weight.shape[0])[None, :]
    ).astype(jnp.bfloat16)
    forward_adapter = jnp.dot(
        pick_home, replica_adapter, preferred_element_type=jnp.float32
    ).astype(jnp.bfloat16)
    slots_out = replicas * pair_cap
    source_mine = lax.dynamic_index_in_dim(source, myself, 0, keepdims=False)
    rank_mine = lax.dynamic_index_in_dim(order_rank, myself, 0, keepdims=False)
    replica_ids = jnp.arange(replicas)
    incoming = (source_mine[:, None, None] == replica_ids[None, :, None]) & (
        rank_mine[:, None, None] == lane_ids[None, None, :]
    )
    incoming = incoming.reshape(replica_slot_count, slots_out).astype(jnp.bfloat16)

    def settle(received):
        flat = received.reshape((slots_out,) + received.shape[2:])
        return jnp.einsum("jp,pxy->jxy", incoming, flat, preferred_element_type=jnp.float32).astype(
            jnp.bfloat16
        )

    def lanes(sent):
        return sent.reshape((replicas, pair_cap) + sent.shape[1:])

    send_rows = jnp.einsum(
        "ph,hrc->prc", pick_home, home_rows, preferred_element_type=jnp.float32
    ).astype(jnp.bfloat16)
    send_up = jnp.einsum(
        "bi,ivx->bvx", forward_adapter, adapter_up_weight, preferred_element_type=jnp.float32
    ).astype(jnp.bfloat16)
    send_down = jnp.einsum(
        "rf,fwh->rwh", forward_adapter, adapter_down_weight, preferred_element_type=jnp.float32
    ).astype(jnp.bfloat16)
    got_rows, got_down, got_up = (
        lax.all_to_all(lanes(send_rows), "replica", split_axis=0, concat_axis=0, tiled=True),
        lax.all_to_all(lanes(send_down), "replica", split_axis=0, concat_axis=0, tiled=True),
        lax.all_to_all(lanes(send_up), "replica", split_axis=0, concat_axis=0, tiled=True),
    )
    block_rows = settle(got_rows)
    local_down = settle(got_down)
    up_slices = settle(got_up)
    partial_value = jnp.einsum(
        "jkd,jrd->jkr", local_down, block_rows, preferred_element_type=jnp.float32
    )
    rank_reduced = lax.psum(partial_value, "tensor").astype(jnp.bfloat16)
    block_count = block_rows.shape[0]
    base_terms = jnp.dot(
        block_rows.reshape(block_count * queued_block_rows, width_dev),
        key_value_weight,
        preferred_element_type=jnp.float32,
    )
    base_key_value = lax.psum_scatter(base_terms, "tensor", scatter_dimension=1, tiled=True)
    output_columns = base_key_value.shape[1]
    adapter_delta = jnp.einsum(
        "abq,abp->aqp", rank_reduced, up_slices, preferred_element_type=jnp.float32
    )
    projected_output = (
        base_key_value.reshape(block_count, queued_block_rows, output_columns)
        + adapter_scale * adapter_delta
    ).astype(jnp.bfloat16)
    return projected_output.reshape(replica_slot_count * queued_block_rows, output_columns)


def solution(mesh):
    return jax.shard_map(
        shards,
        mesh=mesh,
        in_specs=(
            P(("groups", "replica"), "tensor"),
            P(("groups", "replica")),
            P("groups", None),
            P("tensor", None),
            P(("groups", "replica"), None, "tensor"),
            P(("groups", "replica"), None, "tensor"),
        ),
        out_specs=P(("groups", "replica"), "tensor"),
        check_vma=False,
    )
```

profile of v0, /device:TPU:0, one launch (start us, length us, event | category | flops | bytes accessed | tf_op | source)
XLA Modules:
  0.0 599.3 jit_solution(757324227681538525)
XLA Ops:
  6.5 0.8 slice_reduce_fusion.1
  7.3 0.1 reshape_squeeze.3
  7.4 0.2 convert_reduce_fusion
  7.7 0.2 fusion.45
  7.9 0.2 select_reduce_fusion
  8.1 0.1 copy.45
  8.2 0.1 eq.120
  8.3 0.1 copy.44
  8.4 0.1 and.47
  8.5 23.8 %fusion.6 = bf16[24,128,2048]{2,0,1:T(8,128)(2,1)} fusion(bf16[24,128,2048]{2,1,0:T(8,128)(2,1)} %bitcast.41, s32[24]{0:T(128)S(1)} %eq.120, pred[24]{0:T(512)(128)(4,1)S(1)} %and.47), kind=kOutput, calls=%fused_computation.7 | convolution fusion | flops 308282496 | bytes 25165944 | tf_op jit(solution)/shard_map/ph,hrc->prc/dot_general | solution.py:63
  32.3 14.5 %copy.47 = bf16[24,128,2048]{2,1,0:T(8,128)(2,1)} copy(bf16[24,128,2048]{2,0,1:T(8,128)(2,1)} %fusion.6) | data formatting | bytes 25165824 | tf_op jit(solution)/shard_map/convert_element_type | solution.py:65
  46.8 6.3 %all-to-all-start = ((bf16[4,6,128,2048]{3,2,1,0:T(8,128)(2,1)}), bf16[4,6,128,2048]{3,2,1,0:T(8,128)(2,1)}, u32[]{:S(2)}, u32[]{:S(2)}) async-start(bf16[4,6,128,2048]{3,2,1,0:T(8,128)(2,1)} %bitcast.39), calls=%async_computation | async-start | bytes 25165824 | tf_op jit(solution)/shard_map/all_to_all | solution.py:73
  53.1 0.3 reduce-scatter.2.cloned.1.call-start
  53.5 274.3 %all-to-all-done = bf16[4,6,128,2048]{3,2,1,0:T(8,128)(2,1)} async-done(((bf16[4,6,128,2048]{3,2,1,0:T(8,128)(2,1)}), bf16[4,6,128,2048]{3,2,1,0:T(8,128)(2,1)}, u32[]{:S(2)}, u32[]{:S(2)}) %all-to-all-start) | async-done | bytes 12582944 | tf_op jit(solution)/shard_map/all_to_all | solution.py:73
  327.8 30.0 %bitcast_convert_fusion = bf16[8,128,2048]{2,0,1:T(8,128)(2,1)} fusion(bf16[4,6,128,2048]{3,2,1,0:T(8,128)(2,1)} %all-to-all-done, pred[8,6]{1,0:T(8,128)(4,1)S(1)} %iota_compare_fusion.4, pred[8,4]{0,1:T(4,128)(4,1)S(1)} %iota_compare_fusion.6), kind=kOutput, calls=%fused_computation.4 | convolution fusion | flops 102760640 | bytes 16777296 | tf_op jit(solution)/shard_map/jp,pxy->jxy/dot_general | solution.py:56
  357.8 4.5 copy.49
  362.3 13.2 %fusion.52 = f32[1024,2048]{1,0:T(8,128)} fusion(bf16[1024,2048]{1,0:T(8,128)(2,1)S(1)} %bitcast.42, bf16[2048,2048]{1,0:T(8,128)(2,1)} %param.9), kind=kOutput, calls=%fused_computation.59 | convolution fusion | flops 8589934592 | bytes 20971520 | tf_op jit(solution)/shard_map/dot_general | solution.py:85
  375.5 0.6 copy-done.3
  376.2 0.2 fusion.23
  376.5 0.6 convolution_convert_fusion.1
  377.1 1.7 copy.56
  378.8 3.6 all-to-all-start.2
  382.4 2.1 convolution_convert_fusion
  384.5 6.2 %copy.51 = bf16[24,64,2048]{2,1,0:T(8,128)(2,1)} copy(bf16[24,64,2048]{2,0,1:T(8,128)(2,1)S(1)} %convolution_convert_fusion) | data formatting | bytes 12582912 | tf_op jit(solution)/shard_map/convert_element_type | solution.py:71
  390.7 28.4 %all-to-all-done.2 = bf16[4,6,64,512]{3,2,1,0:T(8,128)(2,1)S(1)} async-done(((bf16[4,6,64,512]{3,2,1,0:T(8,128)(2,1)}), bf16[4,6,64,512]{3,2,1,0:T(8,128)(2,1)S(1)}, u32[]{:S(2)}, u32[]{:S(2)}) %all-to-all-start.2) | async-done | bytes 1572896 | tf_op jit(solution)/shard_map/all_to_all | solution.py:75
  419.1 5.5 all-to-all-start.1
  424.6 1.4 fusion.20
  426.0 136.2 %all-to-all-done.1 = bf16[4,6,64,2048]{3,2,1,0:T(8,128)(2,1)} async-done(((bf16[4,6,64,2048]{3,2,1,0:T(8,128)(2,1)}), bf16[4,6,64,2048]{3,2,1,0:T(8,128)(2,1)}, u32[]{:S(2)}, u32[]{:S(2)}) %all-to-all-start.1) | async-done | bytes 6291488 | tf_op jit(solution)/shard_map/all_to_all | solution.py:74
  562.2 9.8 %bitcast_convert_fusion.1 = bf16[8,64,2048]{2,0,1:T(8,128)(2,1)S(1)} fusion(bf16[4,6,64,2048]{3,2,1,0:T(8,128)(2,1)} %all-to-all-done.1, pred[8,6]{1,0:T(8,128)(4,1)S(1)} %iota_compare_fusion.4, pred[8,4]{0,1:T(4,128)(4,1)S(1)} %iota_compare_fusion.6), kind=kOutput, calls=%fused_computation.9 | convolution fusion | flops 51380416 | bytes 8388688 | tf_op jit(solution)/shard_map/jp,pxy->jxy/dot_general | solution.py:56
  572.1 3.4 fusion.15
  575.4 13.5 %all-reduce.1 = bf16[8,64,128]{2,1,0:T(8,128)(2,1)S(1)} all-reduce(f32[8,64,128]{2,1,0:T(8,128)S(1)} %fusion.15), channel_id=1, replica_groups=mesh['groups'=2,'replica'=4,'tensor'=4] {'tensor'}, use_global_device_ids=true, to_apply=%region_4.5 | all-reduce | flops 65536 | bytes 393216 | tf_op jit(solution)/shard_map/psum | solution.py:83
  589.0 3.1 add_convert_fusion
  (15 shorter events, 0.3 us)
Async XLA Ops:
  6.5 375.8 %copy-start = (bf16[4,64,2048]{2,1,0:T(8,128)(2,1)S(1)}, bf16[4,64,2048]{2,1,0:T(8,128)(2,1)}, u32[]{:S(2)}) copy-start(bf16[4,64,2048]{2,1,0:T(8,128)(2,1)} %param.10) | copy-start | bytes 3145732
  46.8 281.0 %all-to-all-start = ((bf16[4,6,128,2048]{3,2,1,0:T(8,128)(2,1)}), bf16[4,6,128,2048]{3,2,1,0:T(8,128)(2,1)}, u32[]{:S(2)}, u32[]{:S(2)}) async-start(bf16[4,6,128,2048]{3,2,1,0:T(8,128)(2,1)} %bitcast.39), calls=%async_computation | async-start | bytes 25165824 | tf_op jit(solution)/shard_map/all_to_all | solution.py:73
  53.1 535.8 %reduce-scatter.2.cloned.1.call-start = ((), (), s32[]{:S(2)}) async-start(), calls=%async_computation.4 | async-start | bytes 10485760 | tf_op jit(solution)/shard_map/reduce_scatter | solution.py:90
  375.5 0.7 copy-start.3
  375.5 1.0 copy-start.2
  378.8 40.3 %all-to-all-start.2 = ((bf16[4,6,64,512]{3,2,1,0:T(8,128)(2,1)}), bf16[4,6,64,512]{3,2,1,0:T(8,128)(2,1)S(1)}, u32[]{:S(2)}, u32[]{:S(2)}) async-start(bf16[4,6,64,512]{3,2,1,0:T(8,128)(2,1)} %bitcast.14), calls=%async_computation.3 | async-start | bytes 3145728 | tf_op jit(solution)/shard_map/all_to_all | solution.py:75
  419.1 143.1 %all-to-all-start.1 = ((bf16[4,6,64,2048]{3,2,1,0:T(8,128)(2,1)}), bf16[4,6,64,2048]{3,2,1,0:T(8,128)(2,1)}, u32[]{:S(2)}, u32[]{:S(2)}) async-start(bf16[4,6,64,2048]{3,2,1,0:T(8,128)(2,1)} %bitcast.40), calls=%async_computation.2 | async-start | bytes 12582912 | tf_op jit(solution)/shard_map/all_to_all | solution.py:74
  562.2 9.8 %copy-start.1 = (bf16[8,128,2048]{2,0,1:T(8,128)(2,1)S(1)}, bf16[8,128,2048]{2,0,1:T(8,128)(2,1)}, u32[]{:S(2)}) copy-start(bf16[8,128,2048]{2,0,1:T(8,128)(2,1)} %bitcast_convert_fusion) | copy-start | bytes 12582916
Sparse Core Ops, SparseCore 0:
  375.7 70.8 reduce-scatter.1
where the time goes:
time: 608 us; the launch traced here: 599 us
  waiting for transfers between devices  439 us (72%)
  matrix products  87.7 us (14%)
  local copies, waits for them, and re-layouts  28.9 us (5%)
  starting transfers between devices  15.7 us (3%)
  between operations  13.9 us (2%)
  blocking collectives  13.5 us (2%)
    all_to_all x1, waiting for transfers between devices, shards(): lax.all_to_all(lanes(send_rows), 'replica', split_axis=0, concat_axis=0,...  274 us
    all_to_all x1, waiting for transfers between devices, shards(): lax.all_to_all(lanes(send_down), 'replica', split_axis=0, concat_axis=0,...  136 us
    dot_general x3, matrix products, settle(): jnp.einsum('jp,pxy->jxy', incoming, flat, preferred_element_type=jnp.floa...  41.3 us
    all_to_all x1, waiting for transfers between devices, shards(): lax.all_to_all(lanes(send_up), 'replica', split_axis=0, concat_axis=0, ti...  28.4 us
    dot_general x1, matrix products, shards(): jnp.einsum('ph,hrc->prc', pick_home, home_rows, preferred_element_type=jn...  23.8 us
    convert_element_type x1, local copies, waits for them, and re-layouts, shards(): send_rows = jnp.einsum('ph,hrc->prc', pick_home, home_rows, preferred_ele...  14.5 us
    psum x1, blocking collectives, shards(): rank_reduced = lax.psum(partial_value, 'tensor').astype(jnp.bfloat16)  13.5 us
    dot_general x1, matrix products, shards(): jnp.dot(block_rows.reshape(block_count * queued_block_rows, width_dev), k...  13.2 us
  transfers between devices with their start and end apart: 4, of which 3 were waited for; matrix products, arithmetic and copies ran while one was open for 4% of the time, Pallas kernels for 0%

commit v1 on v0

--- a/solution.py
+++ b/solution.py
@@ -1,9 +1,323 @@
+import functools
+
 import jax
 import jax.numpy as jnp
 from jax import lax
+from jax.experimental import pallas as pl
+from jax.experimental.pallas import tpu as pltpu
 from jax.sharding import PartitionSpec as P
 
 adapter_scale = 0.5
+PAIR = 2
+KEEP = 4
+
+
+def fused_kernel(
+    sizes,
+    plan_ref,
+    adapter_ref,
+    rows_hbm,
+    weight_hbm,
+    down_hbm,
+    up_hbm,
+    out_ref,
+    rows,
+    weight,
+    down,
+    down_t,
+    up,
+    lhs,
+    send_a,
+    recv_a,
+    own,
+    keep,
+    send_b,
+    recv_b,
+    send_z,
+    lanes,
+    load_sem,
+    up_send_sem,
+    up_recv_sem,
+    a_send_sem,
+    a_recv_sem,
+    b_send_sem,
+    b_recv_sem,
+    z_send_sem,
+    z_recv_sem,
+):
+    replicas, cap, pair_cap, block, adapters, rank = sizes
+    columns = out_ref.shape[1]
+    step_rows = PAIR * block
+    per_dest = pair_cap // PAIR
+    remote_steps = (replicas - 1) * per_dest
+    steps = replicas * per_dest
+
+    me = lax.axis_index("replica")
+    t = lax.axis_index("tensor")
+    chip, core = t // 2, t % 2
+    sibling = chip * 2 + (1 - core)
+    across = (1 - chip) * 2 + core
+    diagonal = (1 - chip) * 2 + (1 - core)
+    roles = (diagonal, sibling, across, t)
+
+    loads = []
+    loads.append(pltpu.make_async_copy(up_hbm, up.at[3], load_sem.at[0]))
+    loads.append(pltpu.make_async_copy(down_hbm, down, load_sem.at[1]))
+    loads.append(pltpu.make_async_copy(rows_hbm, rows, load_sem.at[2]))
+    for role in range(4):
+        start = pl.multiple_of(roles[role] * columns, columns)
+        loads.append(
+            pltpu.make_async_copy(
+                weight_hbm.at[:, pl.ds(start, columns)], weight.at[role], load_sem.at[3 + role]
+            )
+        )
+    for load in loads:
+        load.start()
+
+    barrier = pltpu.get_barrier_semaphore()
+    for peer in (sibling, across):
+        pl.semaphore_signal(
+            barrier, inc=1, device_id={"tensor": peer}, device_id_type=pl.DeviceIdType.MESH
+        )
+    for off in range(1, replicas):
+        pl.semaphore_signal(
+            barrier,
+            inc=1,
+            device_id={"replica": lax.rem(me + off, replicas)},
+            device_id_type=pl.DeviceIdType.MESH,
+        )
+    pl.semaphore_wait(barrier, 2 + replicas - 1)
+
+    def to_tensor(src, dst, send, recv, peer):
+        return pltpu.make_async_remote_copy(
+            src_ref=src,
+            dst_ref=dst,
+            send_sem=send,
+            recv_sem=recv,
+            device_id={"tensor": peer},
+            device_id_type=pl.DeviceIdType.MESH,
+        )
+
+    loads[0].wait()
+    up_across = to_tensor(up.at[3], up.at[2], up_send_sem.at[0], up_recv_sem.at[0], across)
+    up_sibling = to_tensor(up.at[3], up.at[1], up_send_sem.at[1], up_recv_sem.at[1], sibling)
+    up_forward = to_tensor(up.at[2], up.at[0], up_send_sem.at[2], up_recv_sem.at[2], sibling)
+    up_across.start()
+    up_sibling.start()
+    loads[1].wait()
+    down_t[...] = down[...].T
+    up_across.wait_recv()
+    up_forward.start()
+    for load in loads[2:]:
+        load.wait()
+    up_sibling.wait_recv()
+    up_forward.wait_recv()
+
+    def copy_a(s):
+        return to_tensor(
+            send_a.at[lax.rem(s, 2)], recv_a.at[s], a_send_sem.at[lax.rem(s, 2)], a_recv_sem.at[s], sibling
+        )
+
+    def copy_b(s):
+        return to_tensor(send_b.at[s], recv_b.at[s], b_send_sem.at[s], b_recv_sem.at[s], across)
+
+    def offset_of(s):
+        return 1 + lax.rem(s, replicas - 1), s // (replicas - 1)
+
+    def copy_z(s):
+        off, k = offset_of(s)
+        return pltpu.make_async_remote_copy(
+            src_ref=send_z.at[s],
+            dst_ref=lanes.at[pl.ds(off * pair_cap + k * PAIR, PAIR)],
+            send_sem=z_send_sem.at[s],
+            recv_sem=z_recv_sem.at[s],
+            device_id={"replica": lax.rem(me + off, replicas)},
+            device_id_type=pl.DeviceIdType.MESH,
+        )
+
+    column_adapter = lax.broadcasted_iota(jnp.int32, (block, adapters * rank), 1) // rank
+
+    def compute(s):
+        off, k = offset_of(s)
+        off = jnp.where(s < remote_steps, off, 0)
+        k = jnp.where(s < remote_steps, k, s - remote_steps)
+        dest = lax.rem(me + off, replicas)
+        count = jnp.int32(0)
+        picked = [jnp.int32(0)] * PAIR
+        for j in range(cap):
+            mine = plan_ref[dest * cap + j, 0] == me
+            home = plan_ref[dest * cap + j, 1]
+            for i in range(PAIR):
+                picked[i] = jnp.where(mine & (count == k * PAIR + i), home, picked[i])
+            count = count + jnp.where(mine, 1, 0)
+        masks = []
+        for i in range(PAIR):
+            lhs[pl.ds(i * block, block), :] = rows[picked[i]]
+            masks.append(column_adapter == adapter_ref[picked[i]])
+        mask = jnp.concatenate(masks, axis=0)
+        shrink = jnp.dot(lhs[...], down_t[...], preferred_element_type=jnp.float32)
+        shrink = jnp.where(mask, shrink * adapter_scale, 0.0)
+        high = shrink.astype(jnp.bfloat16)
+        low = (shrink - high.astype(jnp.float32)).astype(jnp.bfloat16)
+
+        def partial(role):
+            return (
+                jnp.dot(lhs[...], weight[role], preferred_element_type=jnp.float32)
+                + jnp.dot(high, up[role], preferred_element_type=jnp.float32)
+                + jnp.dot(low, up[role], preferred_element_type=jnp.float32)
+            )
+
+        slot = lax.rem(s, 2)
+
+        @pl.when(s >= 2)
+        def _():
+            copy_a(s - 2).wait_send()
+
+        send_a[slot, 0] = partial(0)
+        send_a[slot, 1] = partial(1)
+        copy_a(s).start()
+        own[slot, 0] = partial(2)
+        own[slot, 1] = partial(3)
+
+    def stage_b(s):
+        copy_a(s).wait_recv()
+        slot = lax.rem(s, 2)
+        send_b[s] = (own[slot, 0] + recv_a[s, 0]).astype(jnp.bfloat16)
+        copy_b(s).start()
+        keep[lax.rem(s, KEEP)] = own[slot, 1] + recv_a[s, 1]
+
+    def stage_c(s):
+        copy_b(s).wait_recv()
+        total = keep[lax.rem(s, KEEP)] + recv_b[s].astype(jnp.float32)
+        total = total.astype(jnp.bfloat16).reshape(PAIR, block, columns)
+
+        @pl.when(s < remote_steps)
+        def _():
+            send_z[s] = total
+            copy_z(s).start()
+
+        @pl.when(s >= remote_steps)
+        def _():
+            lanes[pl.ds((s - remote_steps) * PAIR, PAIR)] = total
+
+    def step(s, _):
+        @pl.when(s < steps)
+        def _():
+            compute(s)
+
+        @pl.when((s >= 1) & (s < steps + 1))
+        def _():
+            stage_b(s - 1)
+
+        @pl.when(s >= KEEP)
+        def _():
+            stage_c(s - KEEP)
+
+        return 0
+
+    lax.fori_loop(0, steps + KEEP, step, 0)
+
+    up_across.wait_send()
+    up_sibling.wait_send()
+    up_forward.wait_send()
+    copy_a(steps - 2).wait_send()
+    copy_a(steps - 1).wait_send()
+
+    def drain_b(s, _):
+        copy_b(s).wait_send()
+        return 0
+
+    lax.fori_loop(0, steps, drain_b, 0)
+
+    def drain_z(s, _):
+        copy_z(s).wait()
+        return 0
+
+    lax.fori_loop(0, remote_steps, drain_z, 0)
+
+    count = [jnp.int32(0)] * replicas
+    for j in range(cap):
+        source = plan_ref[me * cap + j, 0]
+        place = jnp.int32(0)
+        for r in range(replicas):
+            here = source == r
+            place = jnp.where(here, lax.rem(me - r + replicas, replicas) * pair_cap + count[r], place)
+            count[r] = count[r] + jnp.where(here, 1, 0)
+        value = lanes[jnp.minimum(place, replicas * pair_cap - 1)]
+        live = jnp.full(value.shape, source, jnp.int32) >= 0
+        out_ref[pl.ds(j * block, block), :] = jnp.where(
+            live, value.astype(jnp.float32), 0.0
+        ).astype(jnp.bfloat16)
+
+
+def fused(
+    normed_hidden_rows,
+    block_adapter_index,
+    transfer_plan,
+    key_value_weight,
+    adapter_down_weight,
+    adapter_up_weight,
+    pair_cap,
+):
+    replicas = lax.axis_size("replica")
+    cap = transfer_plan.shape[0] // replicas
+    home = block_adapter_index.shape[0]
+    width = normed_hidden_rows.shape[1]
+    block = normed_hidden_rows.shape[0] // home
+    adapters, rank, columns = adapter_up_weight.shape
+    adapter_rows = adapters * rank
+    steps = replicas * pair_cap // PAIR
+    remote_steps = (replicas - 1) * pair_cap // PAIR
+    step_rows = PAIR * block
+    smem = pl.BlockSpec(memory_space=pltpu.SMEM)
+    hbm = pl.BlockSpec(memory_space=pl.ANY)
+    dma = pltpu.SemaphoreType.DMA
+    sizes = (replicas, cap, pair_cap, block, adapters, rank)
+    flops = 2 * steps * step_rows * width * 4 * columns
+    return pl.pallas_call(
+        functools.partial(fused_kernel, sizes),
+        out_shape=jax.ShapeDtypeStruct((cap * block, columns), jnp.bfloat16),
+        in_specs=[smem, smem, hbm, hbm, hbm, hbm],
+        out_specs=pl.BlockSpec(memory_space=pltpu.VMEM),
+        scratch_shapes=[
+            pltpu.VMEM((home, block, width), jnp.bfloat16),
+            pltpu.VMEM((4, width, columns), jnp.bfloat16),
+            pltpu.VMEM((adapter_rows, width), jnp.bfloat16),
+            pltpu.VMEM((width, adapter_rows), jnp.bfloat16),
+            pltpu.VMEM((4, adapter_rows, columns), jnp.bfloat16),
+            pltpu.VMEM((step_rows, width), jnp.bfloat16),
+            pltpu.VMEM((2, 2, step_rows, columns), jnp.float32),
+            pltpu.VMEM((steps, 2, step_rows, columns), jnp.float32),
+            pltpu.VMEM((2, 2, step_rows, columns), jnp.float32),
+            pltpu.VMEM((KEEP, step_rows, columns), jnp.float32),
+            pltpu.VMEM((steps, step_rows, columns), jnp.bfloat16),
+            pltpu.VMEM((steps, step_rows, columns), jnp.bfloat16),
+            pltpu.VMEM((remote_steps, PAIR, block, columns), jnp.bfloat16),
+            pltpu.VMEM((replicas * pair_cap, block, columns), jnp.bfloat16),
+            dma((7,)),
+            dma((3,)),
+            dma((3,)),
+            dma((2,)),
+            dma((steps,)),
+            dma((steps,)),
+            dma((steps,)),
+            dma((remote_steps,)),
+            dma((remote_steps,)),
+        ],
+        compiler_params=pltpu.CompilerParams(
+            collective_id=0, has_side_effects=True, vmem_limit_bytes=62 * 1024 * 1024
+        ),
+        cost_estimate=pl.CostEstimate(
+            flops=flops, bytes_accessed=2 * normed_hidden_rows.size, transcendentals=0
+        ),
+    )(
+        transfer_plan,
+        block_adapter_index,
+        normed_hidden_rows.reshape(home, block, width),
+        key_value_weight,
+        adapter_down_weight.reshape(adapter_rows, width),
+        adapter_up_weight.reshape(adapter_rows, columns),
+    )
 
 
 def shards(
@@ -18,6 +332,16 @@
     myself = lax.axis_index("replica")
     replica_slot_count = transfer_plan.shape[0] // replicas
     pair_cap = (3 * replica_slot_count + replicas - 1) // replicas
+    if replicas == 4 and lax.axis_size("tensor") == 4 and pair_cap % PAIR == 0:
+        return fused(
+            normed_hidden_rows,
+            block_adapter_index,
+            transfer_plan,
+            key_value_weight,
+            adapter_down_weight,
+            adapter_up_weight,
+            pair_cap,
+        )
     home_count = block_adapter_index.shape[0]
     queued_block_rows = normed_hidden_rows.shape[0] // home_count
     width_dev = normed_hidden_rows.shape[1]

time: 608 us -> 106 us (0.17)
  the two profiles are of different devices: /device:TPU:0 before, /device:TPU:13 now
where the time goes in v1:
time: 106 us
  Pallas kernels  102 us (96%)
  local copies, waits for them, and re-layouts  3.63 us (3%)
    pallas_call x1, Pallas kernels, fused(): pl.pallas_call(functools.partial(fused_kernel, sizes), out_shape=jax.Shap...  102 us
    unnamed x2, local copies, waits for them, and re-layouts  3.63 us

profile of v1, /device:TPU:13, one launch (start us, length us, event | category | flops | bytes accessed | tf_op | source)
XLA Modules:
  0.0 105.7 jit_solution(16685183077410687519)
XLA Ops:
  0.0 1.4 %copy.7.plan_ref = s32[32,2]{1,0:T(8,128)} copy(s32[32,2]{0,1:T(2,128)} %param.8) | data formatting | bytes 512 | tf_op args[2]
  1.4 102.0 %shard_map.64 = bf16[1024,512]{1,0:T(8,128)(2,1)} custom-call(s32[32,2]{1,0:T(8,128)} %copy.7.plan_ref, s32[24]{0:T(128)} %adapter_ref.1, bf16[24,128,2048]{2,1,0:T(8,128)(2,1)} %bitcast.3, bf16[2048,2048]{1,0:T(8,128)(2,1)} %weight_hbm.1, bf16[256,2048]{1,0:T(8,128)(2,1)} %bitcast.4, bf16[256,512]{1,0:T(8,128)(2,1)} %bitcast.5), custom_call_target="tpu_custom_call" | custom-call | flops 25769803776 | bytes 12582912 | tf_op jit(solution)/shard_map/pallas_call | solution.py:277
  103.4 2.3 %copy.9 = bf16[1024,512]{1,0:T(8,128)(2,1)} copy(bf16[1024,512]{1,0:T(8,128)(2,1)} %shard_map.64) | data formatting | bytes 2097152

commit v2 on v1

--- a/solution.py
+++ b/solution.py
@@ -35,6 +35,7 @@
     recv_b,
     send_z,
     lanes,
+    relay,
     load_sem,
     up_send_sem,
     up_recv_sem,
@@ -44,6 +45,7 @@
     b_recv_sem,
     z_send_sem,
     z_recv_sem,
+    relay_sem,
 ):
     replicas, cap, pair_cap, block, adapters, rank = sizes
     columns = out_ref.shape[1]
@@ -121,35 +123,59 @@
     def copy_b(s):
         return to_tensor(send_b.at[s], recv_b.at[s], b_send_sem.at[s], b_recv_sem.at[s], across)
 
-    def offset_of(s):
-        return 1 + lax.rem(s, replicas - 1), s // (replicas - 1)
+    half = me // 2
+    partner = me + 1 - 2 * (me % 2)
+    inner = (me == 1) | (me == 2)
+
+    def place_of(s):
+        c = s % 3
+        dest = jnp.where(c < 2, (1 - half) * 2 + c, partner)
+        return jnp.where(s < remote_steps, dest, me), jnp.where(
+            s < remote_steps, s // 3, s - remote_steps
+        )
+
+    def relayed(s):
+        return (s >= 3) & (s < remote_steps) & (s % 3 < 2)
+
+    def lanes_of(source, k):
+        return lanes.at[pl.ds(source * pair_cap + k * PAIR, PAIR)]
+
+    def to_replica(src, dst, send, recv, peer):
+        return pltpu.make_async_remote_copy(
+            src_ref=src,
+            dst_ref=dst,
+            send_sem=send,
+            recv_sem=recv,
+            device_id={"replica": peer},
+            device_id_type=pl.DeviceIdType.MESH,
+        )
 
     def copy_z(s):
-        off, k = offset_of(s)
-        return pltpu.make_async_remote_copy(
-            src_ref=send_z.at[s],
-            dst_ref=lanes.at[pl.ds(off * pair_cap + k * PAIR, PAIR)],
-            send_sem=z_send_sem.at[s],
-            recv_sem=z_recv_sem.at[s],
-            device_id={"replica": lax.rem(me + off, replicas)},
-            device_id_type=pl.DeviceIdType.MESH,
-        )
-
-    column_adapter = lax.broadcasted_iota(jnp.int32, (block, adapters * rank), 1) // rank
-
-    def compute(s):
-        off, k = offset_of(s)
-        off = jnp.where(s < remote_steps, off, 0)
-        k = jnp.where(s < remote_steps, k, s - remote_steps)
-        dest = lax.rem(me + off, replicas)
+        dest, k = place_of(s)
+        return to_replica(
+            send_z.at[s], lanes_of(me, k), z_send_sem.at[s], z_recv_sem.at[me * per_dest + k], dest
+        )
+
+    def copy_relay(s):
+        return to_replica(send_z.at[s], relay.at[s], z_send_sem.at[s], relay_sem.at[s], partner)
+
+    def lane_of(s, i):
+        dest, k = place_of(s)
         count = jnp.int32(0)
-        picked = [jnp.int32(0)] * PAIR
+        home = jnp.int32(0)
+        live = jnp.int32(0)
         for j in range(cap):
             mine = plan_ref[dest * cap + j, 0] == me
-            home = plan_ref[dest * cap + j, 1]
-            for i in range(PAIR):
-                picked[i] = jnp.where(mine & (count == k * PAIR + i), home, picked[i])
+            here = mine & (count == k * PAIR + i)
+            home = jnp.where(here, plan_ref[dest * cap + j, 1], home)
+            live = jnp.where(here, 1, live)
             count = count + jnp.where(mine, 1, 0)
+        return home, live
+
+    column_adapter = lax.broadcasted_iota(jnp.int32, (block, adapters * rank), 1) // rank
+
+    def compute(s):
+        picked = [lane_of(s, i)[0] for i in range(PAIR)]
         masks = []
         for i in range(PAIR):
             lhs[pl.ds(i * block, block), :] = rows[picked[i]]
@@ -194,11 +220,29 @@
         @pl.when(s < remote_steps)
         def _():
             send_z[s] = total
+
+        @pl.when((s < remote_steps) & jnp.logical_not(relayed(s)))
+        def _():
             copy_z(s).start()
 
+        @pl.when(relayed(s) & jnp.logical_not(inner))
+        def _():
+            copy_relay(s).start()
+
         @pl.when(s >= remote_steps)
         def _():
-            lanes[pl.ds((s - remote_steps) * PAIR, PAIR)] = total
+            lanes[pl.ds(me * pair_cap + (s - remote_steps) * PAIR, PAIR)] = total
+
+    def stage_d(s):
+        @pl.when(relayed(s) & inner)
+        def _():
+            copy_relay(s).wait_recv()
+            for i in range(PAIR):
+                value = send_z[s, i].astype(jnp.float32)
+                live = jnp.full(value.shape, lane_of(s, i)[1], jnp.int32) > 0
+                other = relay[s, i].astype(jnp.float32)
+                send_z[s, i] = jnp.where(live, value, other).astype(jnp.bfloat16)
+            copy_z(s).start()
 
     def step(s, _):
         @pl.when(s < steps)
@@ -212,6 +256,10 @@
         @pl.when(s >= KEEP)
         def _():
             stage_c(s - KEEP)
+
+        @pl.when(s >= KEEP + 2)
+        def _():
+            stage_d(s - KEEP - 2)
 
         return 0
 
@@ -230,10 +278,22 @@
     lax.fori_loop(0, steps, drain_b, 0)
 
     def drain_z(s, _):
-        copy_z(s).wait()
+        copy_z(s).wait_send()
         return 0
 
     lax.fori_loop(0, remote_steps, drain_z, 0)
+
+    def arrived(source, k):
+        to_replica(
+            send_z.at[0], lanes_of(source, k), z_send_sem.at[0], z_recv_sem.at[source * per_dest + k], partner
+        ).wait_recv()
+
+    far_inner = jnp.where(half == 0, 2, 1)
+    far_end = jnp.where(half == 0, 3, 0)
+    for k in range(per_dest):
+        arrived(partner, k)
+        arrived(far_inner, k)
+    arrived(far_end, 0)
 
     count = [jnp.int32(0)] * replicas
     for j in range(cap):
@@ -241,7 +301,12 @@
         place = jnp.int32(0)
         for r in range(replicas):
             here = source == r
-            place = jnp.where(here, lax.rem(me - r + replicas, replicas) * pair_cap + count[r], place)
+            direct = r * pair_cap + count[r]
+            if r in (0, 3):
+                through = (1 if r == 0 else 2) * pair_cap + count[r]
+                by_relay = (half != r // 2) & (count[r] >= PAIR)
+                direct = jnp.where(by_relay, through, direct)
+            place = jnp.where(here, direct, place)
             count[r] = count[r] + jnp.where(here, 1, 0)
         value = lanes[jnp.minimum(place, replicas * pair_cap - 1)]
         live = jnp.full(value.shape, source, jnp.int32) >= 0
@@ -294,6 +359,7 @@
             pltpu.VMEM((steps, step_rows, columns), jnp.bfloat16),
             pltpu.VMEM((remote_steps, PAIR, block, columns), jnp.bfloat16),
             pltpu.VMEM((replicas * pair_cap, block, columns), jnp.bfloat16),
+            pltpu.VMEM((remote_steps, PAIR, block, columns), jnp.bfloat16),
             dma((7,)),
             dma((3,)),
             dma((3,)),
@@ -302,6 +368,7 @@
             dma((steps,)),
             dma((steps,)),
             dma((remote_steps,)),
+            dma((steps,)),
             dma((remote_steps,)),
         ],
         compiler_params=pltpu.CompilerParams(
@@ -332,7 +399,11 @@
     myself = lax.axis_index("replica")
     replica_slot_count = transfer_plan.shape[0] // replicas
     pair_cap = (3 * replica_slot_count + replicas - 1) // replicas
-    if replicas == 4 and lax.axis_size("tensor") == 4 and pair_cap % PAIR == 0:
+    one_full_source = (
+        block_adapter_index.shape[0] == replicas * pair_cap
+        and replica_slot_count - pair_cap <= PAIR
+    )
+    if replicas == 4 and lax.axis_size("tensor") == 4 and pair_cap % PAIR == 0 and one_full_source:
         return fused(
             normed_hidden_rows,
             block_adapter_index,

time: 106 us -> 95.7 us (0.903)
  the two profiles are of different devices: /device:TPU:13 before, /device:TPU:0 now
where the time goes in v2:
time: 95.7 us; the launch traced here: 95.2 us
  Pallas kernels  91.6 us (96%)
  local copies, waits for them, and re-layouts  3.63 us (4%)
    pallas_call x1, Pallas kernels, fused(): pl.pallas_call(functools.partial(fused_kernel, sizes), out_shape=jax.Shap...  91.6 us
    unnamed x2, local copies, waits for them, and re-layouts  3.63 us

profile of v2, /device:TPU:0, one launch (start us, length us, event | category | flops | bytes accessed | tf_op | source)
XLA Modules:
  0.0 95.2 jit_solution(16813225398503551289)
XLA Ops:
  0.0 1.4 %copy.7.plan_ref = s32[32,2]{1,0:T(8,128)} copy(s32[32,2]{0,1:T(2,128)} %param.8) | data formatting | bytes 512 | tf_op args[2]
  1.4 91.6 %shard_map.64 = bf16[1024,512]{1,0:T(8,128)(2,1)} custom-call(s32[32,2]{1,0:T(8,128)} %copy.7.plan_ref, s32[24]{0:T(128)} %adapter_ref.1, bf16[24,128,2048]{2,1,0:T(8,128)(2,1)} %bitcast.3, bf16[2048,2048]{1,0:T(8,128)(2,1)} %weight_hbm.1, bf16[256,2048]{1,0:T(8,128)(2,1)} %bitcast.4, bf16[256,512]{1,0:T(8,128)(2,1)} %bitcast.5), custom_call_target="tpu_custom_call" | custom-call | flops 25769803776 | bytes 12582912 | tf_op jit(solution)/shard_map/pallas_call | solution.py:342
  93.0 2.3 %copy.9 = bf16[1024,512]{1,0:T(8,128)(2,1)} copy(bf16[1024,512]{1,0:T(8,128)(2,1)} %shard_map.64) | data formatting | bytes 2097152

commit v3 on v2

--- a/solution.py
+++ b/solution.py
@@ -245,21 +245,21 @@
             copy_z(s).start()
 
     def step(s, _):
+        @pl.when((s >= 1) & (s < steps + 1))
+        def _():
+            stage_b(s - 1)
+
+        @pl.when(s >= KEEP)
+        def _():
+            stage_c(s - KEEP)
+
+        @pl.when(s >= KEEP + 2)
+        def _():
+            stage_d(s - KEEP - 2)
+
         @pl.when(s < steps)
         def _():
             compute(s)
-
-        @pl.when((s >= 1) & (s < steps + 1))
-        def _():
-            stage_b(s - 1)
-
-        @pl.when(s >= KEEP)
-        def _():
-            stage_c(s - KEEP)
-
-        @pl.when(s >= KEEP + 2)
-        def _():
-            stage_d(s - KEEP - 2)
 
         return 0
 

time: 95.7 us -> 93.6 us (0.978)
  Pallas kernels: 91.6 us -> 89.7 us
    pallas_call x1, Pallas kernels: 91.6 us -> 89.7 us  [fused(): pl.pallas_call(functools.partial(fused_kernel, sizes), out_shape=jax.Shap...]
where the time goes in v3:
time: 93.6 us; the launch traced here: 93.3 us
  Pallas kernels  89.7 us (96%)
  local copies, waits for them, and re-layouts  3.63 us (4%)
    pallas_call x1, Pallas kernels, fused(): pl.pallas_call(functools.partial(fused_kernel, sizes), out_shape=jax.Shap...  89.7 us
    unnamed x2, local copies, waits for them, and re-layouts  3.63 us

profile of v3, /device:TPU:0, one launch (start us, length us, event | category | flops | bytes accessed | tf_op | source)
XLA Modules:
  0.0 93.3 jit_solution(4561033543449677349)
XLA Ops:
  0.0 1.4 %copy.7.plan_ref = s32[32,2]{1,0:T(8,128)} copy(s32[32,2]{0,1:T(2,128)} %param.8) | data formatting | bytes 512 | tf_op args[2]
  1.4 89.7 %shard_map.64 = bf16[1024,512]{1,0:T(8,128)(2,1)} custom-call(s32[32,2]{1,0:T(8,128)} %copy.7.plan_ref, s32[24]{0:T(128)} %adapter_ref.1, bf16[24,128,2048]{2,1,0:T(8,128)(2,1)} %bitcast.3, bf16[2048,2048]{1,0:T(8,128)(2,1)} %weight_hbm.1, bf16[256,2048]{1,0:T(8,128)(2,1)} %bitcast.4, bf16[256,512]{1,0:T(8,128)(2,1)} %bitcast.5), custom_call_target="tpu_custom_call" | custom-call | flops 25769803776 | bytes 12582912 | tf_op jit(solution)/shard_map/pallas_call | solution.py:342
  91.1 2.3 %copy.9 = bf16[1024,512]{1,0:T(8,128)(2,1)} copy(bf16[1024,512]{1,0:T(8,128)(2,1)} %shard_map.64) | data formatting | bytes 2097152
